TPU v7x, 32 devices: a whole 2x2x4 slice. The times are simulated.
32 devices in a mesh: rows: 8 (over y, x, core), heads: 4 (over z).
Axes of the slice: x: 2, y: 2, z: 4, core: 2. Of those that a mesh axis runs over, the one named last changes fastest.
Arguments:
- token_ids: int32 [32, 1024], P('rows'), may hold values from 0 to 50271
- segment_ids: int32 [32, 1024], P('rows'), may hold values from 0 to 7, never falling along the last dimension, each value on 1 to 256 neighbouring positions
- row_fill: int32 [32], P('rows'), may hold values from 512 to 1024
- task_ids: int32 [32, 8], P('rows'), may hold values from 0 to 7
- labels: int32 [32, 8], P('rows'), may hold values from 0 to 2
- task_weights: int32 [8], replicated, may hold values from 1 to 4
- word_table: bfloat16 [50272, 1024], P('heads'), may hold values from -6 to 6
- position_table: bfloat16 [258, 1024], replicated, may hold values from -6 to 6
- norm_gains: float32 [3, 1024], replicated, may hold values from 0.5 to 1.5
- norm_biases: float32 [3, 1024], replicated, may hold values from -2 to 2
- dense_biases: float32 [4, 1024], replicated, may hold values from -2 to 2
- qkv_weight: bfloat16 [1024, 3072], replicated, may hold values from -0.1875 to 0.1875
- out_weight: bfloat16 [1024, 1024], replicated, may hold values from -0.5 to 0.5
- ffn_in: bfloat16 [1024, 4096], replicated, may hold values from -0.1875 to 0.1875
- ffn_bias: float32 [4096], replicated, may hold values from -2 to 2
- ffn_out: bfloat16 [4096, 1024], replicated, may hold values from -0.09375 to 0.09375
- vera_a: bfloat16 [1024, 1024], replicated, may hold values from -0.1875 to 0.1875
- vera_b: bfloat16 [1024, 1024], replicated, may hold values from -0.1875 to 0.1875
- scale_d: float32 [2, 1024], replicated, may hold values from 0.05 to 0.5
- scale_b: float32 [2, 1024], replicated, may hold values from -4 to 4
- task_heads: float32 [8, 3, 1024], replicated, may hold values from -0.1875 to 0.1875
- mom_d: float32 [2, 1024], replicated, may hold values from -0.75 to 0.75
- mom_b: float32 [2, 1024], replicated, may hold values from -0.75 to 0.75
- mom_heads: float32 [8, 3, 1024], replicated, may hold values from -4 to 4
- avg_d: float32 [2, 1024], replicated, may hold values from 0.05 to 0.5
- avg_b: float32 [2, 1024], replicated, may hold values from -4 to 4
- avg_heads: float32 [8, 3, 1024], replicated, may hold values from -0.1875 to 0.1875
Outputs:
- loss: float32 [], replicated
- new_mom_d: float32 [2, 1024], replicated
- new_mom_b: float32 [2, 1024], replicated
- new_mom_heads: float32 [8, 3, 1024], replicated
- new_d: float32 [2, 1024], replicated
- new_b: float32 [2, 1024], replicated
- new_heads: float32 [8, 3, 1024], replicated
- new_avg_d: float32 [2, 1024], replicated
- new_avg_b: float32 [2, 1024], replicated
- new_avg_heads: float32 [8, 3, 1024], replicated
- heads_low: bfloat16 [8, 3, 1024], replicated
- stats: float32 [2], replicated
Inputs may be any that keep to these rules, and one draw needn't show every extreme that they name: `segment_ids`: in each row segment numbers start at 0, never fall, take every value below 8 and no segment has more than 256 slots.
All inputs are finite; a program needn't handle non-finite values.
Results may differ from a plain program's by a relative error of at most 0.008.
Values may be sent and summed in bfloat16 or wider, within the bound.
A program may use at most 256 MiB of HBM per device.

v0:
```python
import functools

import jax
import jax.numpy as jnp
from jax import lax
from jax.experimental import pallas as pl
from jax.experimental.pallas import tpu as pltpu
from jax.sharding import PartitionSpec as P

HEADS = 16
HDIM = 64
TASKS = 8
CLASSES = 3
SEGS = 8
LANES = 128
CHUNKS = 4
BLK = 256
GROUP = 128
SUB = 2
FT = 1024
UNROLL = 8
EPSILON = 1e-05
MOMENTUM = 0.9
AVERAGE = 0.8
RATE_D = 5.0
RATE_B = 20.0
RATE_HEADS = 0.3
NEG = -1e30
BF = jnp.bfloat16
F32 = jnp.float32
MESH = pl.DeviceIdType.MESH


def mm(left, right):
    return jnp.dot(left, right, preferred_element_type=F32)


def mm_t(left, right):
    return lax.dot_general(left, right, (((1,), (1,)), ((), ())), preferred_element_type=F32)


def mm_l(left, right):
    return lax.dot_general(left, right, (((0,), (0,)), ((), ())), preferred_element_type=F32)


def normed(values):
    centred = values - jnp.mean(values, -1, keepdims=True)
    rstd = lax.rsqrt(jnp.mean(centred * centred, -1, keepdims=True) + EPSILON)
    return centred * rstd, rstd


def norm_back(hat, rstd, gain, grad):
    scaled = grad * gain
    return rstd * (
        scaled
        - jnp.mean(scaled, -1, keepdims=True)
        - hat * jnp.mean(scaled * hat, -1, keepdims=True)
    )


def iota(shape, dim):
    return lax.broadcasted_iota(jnp.int32, shape, dim)


def update(weight, grad, moment, average, rate):
    moment_new = MOMENTUM * moment + grad
    weight_new = weight - rate * (grad + MOMENTUM * moment_new)
    return (moment_new, weight_new, AVERAGE * average + (1.0 - AVERAGE) * weight_new)


def gather_kernel(
    cfg, fill, ids, seg, words, x_out, lead_out,
    listv, lists, code, lead, list_sem, buf_sem, out_sem, *big,
):
    R, S, V = cfg
    D = x_out.shape[1]
    PER = S // BLK
    NB = R * PER
    HALVES = BLK // LANES
    bufs, stages = big[:NB], big[NB:]
    z = lax.axis_index("heads")
    slot = iota((1, S), 1)
    lane = iota((1, LANES), 1)
    jcol = iota((SEGS, 1), 0)
    row8 = iota((8, 1), 0)

    local = ids[...] - z * V
    segs = seg[...]
    fills = jnp.zeros((R, 1), jnp.int32)
    for r in range(R):
        fills = jnp.where(iota((R, 1), 0) == r, fill[r], fills)
    first = (slot == 0) | (segs != pltpu.roll(segs, 1, 1))
    need = (local >= 0) & (local < V) & (first | (slot < fills))
    need_f = need.astype(F32)
    upper = (iota((LANES, LANES), 0) <= iota((LANES, LANES), 1)).astype(F32).astype(BF)
    tiles = [need_f[:, LANES * k : LANES * (k + 1)] for k in range(S // LANES)]
    prefix = mm(jnp.concatenate(tiles, 0).astype(BF), upper)
    count_row = jnp.zeros((1, LANES), F32)
    begins = []
    for r in range(R):
        seg_row = segs[r : r + 1, :]
        starts = jnp.sum((seg_row < jcol).astype(jnp.int32), 1, keepdims=True)
        begins.append(starts)
        for p in range(PER):
            b = r * PER + p
            here = slice(BLK * p, BLK * (p + 1))
            runs, total = [], jnp.zeros((1, 1), F32)
            for h in range(HALVES):
                at = (HALVES * p + h) * R + r
                runs.append(prefix[at : at + 1] + total)
                total = total + prefix[at : at + 1, LANES - 1 :]
            wanted = need_f[r : r + 1, here] > 0.0
            rank = jnp.where(wanted, jnp.concatenate(runs, 1).astype(jnp.int32) - 1, -1)
            word = local[r : r + 1, here]
            key = jnp.where(wanted, (rank & (GROUP - 1)) * SUB + (word & (SUB - 1)), -1)
            spots = (iota((GROUP * SUB, 1), 0) == key).astype(F32).astype(BF)
            marks = jnp.where((rank // GROUP) == row8, iota((1, BLK), 1) + 1, 0).astype(F32).astype(BF)
            code[b] = mm_t(marks, spots)
            spots = (iota((LANES, 1), 0) == jnp.where(wanted, rank & (LANES - 1), -1)).astype(F32).astype(BF)
            tile = word // SUB
            plane = jnp.where(row8 < HALVES, tile & 255, tile // 256)
            plane = jnp.where(((rank // LANES) == (row8 & (HALVES - 1))) & (row8 < 2 * HALVES), plane, 0)
            both = mm_t(plane.astype(F32).astype(BF), spots)
            both = both[0:HALVES] + 256.0 * both[HALVES : 2 * HALVES]
            listv[HALVES * b : HALVES * (b + 1), :] = both.astype(jnp.int32)
            count_row = jnp.where(lane == b, total, count_row)
    listv[HALVES * NB :, :] = jnp.broadcast_to(count_row.astype(jnp.int32), (8, LANES))
    to_scalar = pltpu.make_async_copy(listv, lists, list_sem.at[0])
    to_scalar.start()
    lead[...] = jnp.zeros_like(lead)
    for b in range(NB):
        bufs[b][0 : GROUP * SUB // 8] = jnp.zeros((GROUP * SUB // 8, 8, D), BF)
    to_scalar.wait()

    def eights(b):
        n = lists[HALVES * NB, b]
        return jnp.where(n <= GROUP, (n + 7) // 8, (n + GROUP - 1) // GROUP * (GROUP // 8))

    def issue(r):
        for p in range(PER):
            b = r * PER + p

            def eight(i, _, b=b, h=0):
                for u in range(8):
                    word = lists[HALVES * b + h, i * 8 + u]
                    pltpu.make_async_copy(
                        words.at[pl.ds(pl.multiple_of(SUB * word, SUB), SUB)],
                        bufs[b].at[h * GROUP * SUB // 8 + i * SUB + u * SUB // 8, pl.ds(u * SUB % 8, SUB)],
                        buf_sem.at[r],
                    ).start()
                return 0

            lax.fori_loop(0, jnp.minimum(eights(b), GROUP // 8), eight, 0)

            @pl.when(lists[HALVES * NB, b] > GROUP)
            def more(eight=eight):
                lax.fori_loop(0, GROUP // 8, functools.partial(eight, h=1), 0)

    def arrive(r):
        total = eights(r * PER)
        for p in range(1, PER):
            total = total + eights(r * PER + p)
        part = bufs[r * PER].at[pl.ds(0, SUB)]

        def eight(i, _):
            pltpu.make_async_copy(part, part, buf_sem.at[r]).wait()
            return 0

        lax.fori_loop(0, total, eight, 0)

    col = iota((BLK, 1), 0) + 1

    def pick(b, g):
        spot = begins[b // PER] - BLK * (b % PER) + 1
        spot = jnp.where((spot >= 1) & (spot <= BLK), spot, -5)
        want = jnp.concatenate([col, spot, jnp.full((8, 1), -5, jnp.int32)], 0).astype(F32)
        one = (want == code[b, pl.ds(g, 1), :]).astype(F32).astype(BF)
        rows = bufs[b][g * GROUP * SUB // 8 : (g + 1) * GROUP * SUB // 8]
        return mm(one, rows.reshape(GROUP * SUB, D))

    def add_lead(b, got):
        rows = slice(b // PER * SEGS, (b // PER + 1) * SEGS)
        lead[rows, :] = lead[rows, :] + got

    def out_copy(b):
        return pltpu.make_async_copy(stages[b % (2 * PER)], x_out.at[pl.ds(b * BLK, BLK)], out_sem.at[b])

    issue(0)
    for r in range(R):
        if r + 1 < R:
            issue(r + 1)
        arrive(r)
        for b in range(r * PER, (r + 1) * PER):
            if b >= 2 * PER:
                out_copy(b - 2 * PER).wait()
            got = pick(b, 0)
            stages[b % (2 * PER)][...] = got[:BLK].astype(BF)
            add_lead(b, got[BLK : BLK + SEGS])

            @pl.when(lists[HALVES * NB, b] > GROUP)
            def more(b=b):
                got = pick(b, 1)
                stages[b % (2 * PER)][...] = stages[b % (2 * PER)][...] + got[:BLK].astype(BF)
                add_lead(b, got[BLK : BLK + SEGS])

            out_copy(b).start()

    lead_out[...] = lead[...].astype(BF)
    for b in range(max(NB - 2 * PER, 0), NB):
        out_copy(b).wait()


def gather(token_ids, segment_ids, row_fill, word_table):
    R, S = token_ids.shape
    V, D = word_table.shape
    PER = S // BLK
    NB = R * PER
    HALVES = BLK // LANES
    if V % SUB:
        word_table = jnp.pad(word_table, ((0, -V % SUB), (0, 0)))
    v, dma = pltpu.VMEM, pltpu.SemaphoreType.DMA
    vm, hbm, sm = (pl.BlockSpec(memory_space=m) for m in (pltpu.VMEM, pl.ANY, pltpu.SMEM))
    return pl.pallas_call(
        functools.partial(gather_kernel, (R, S, V)),
        out_shape=(jax.ShapeDtypeStruct((R * S, D), BF), jax.ShapeDtypeStruct((R * SEGS, D), BF)),
        in_specs=[sm, vm, vm, hbm],
        out_specs=(hbm, vm),
        scratch_shapes=[
            v((HALVES * NB + 8, LANES), jnp.int32),
            pltpu.SMEM((HALVES * NB + 8, LANES), jnp.int32), v((NB, 8, GROUP * SUB), F32),
            v((R * SEGS, D), F32), dma((1,)), dma((R,)), dma((NB,)),
            *[v((BLK * SUB // 8, 8, D), BF)] * NB, *[v((BLK, D), BF)] * (2 * PER),
        ],
        compiler_params=pltpu.CompilerParams(vmem_limit_bytes=60 * 1024 * 1024),
    )(row_fill, token_ids, segment_ids, word_table)


def step_kernel(
    cfg,
    fill, task_w, ids, seg, tasks, labels, lead_out, gains, shifts, biases, bias_in, scale_d, scale_b, table,
    x_h, place_h, qkv_h, out_h, fin_h, fout_h, va_h, vb_h,
    heads_sum, small_sum,
    x, qkv, outw, fin, fout, va, vb,
    place, places, lead_in, seg_eff, starts_s, xz_s, latent_s, eq_s, qk, expo, ub, ua, ev, pack, st, st_in, pk, pk_in,
    act, slope, gh, tab, lse_out, lse_in, gpk, gpk_in, dlt_out, dlt_in, g_in, zq, zacc, zb, gq_s, fx,
    cnt_out, cnt_in, hs, h_in, hr, hr_in, ag, late, lz_in, lr, lr_in,
    load_sem, x_sem, e1_s, e1_r, cnt_ss, cnt_rs, rs_s, rs_r, g_s, g_r, h_ss, h_rs, hr_ss, hr_rs, ag_ss, ag_rs,
    lz_ss, lz_rs, lr_ss, lr_rs,
):
    R, S, G, NR, V = cfg
    D = x.shape[1]
    FF = fin.shape[1]
    PAIRS = HEADS // 2
    L = R * SEGS
    z = lax.axis_index("heads")
    rw = lax.axis_index("rows")
    own_r = lax.rem(z, R)

    def x_load(r):
        rows = pl.ds(pl.multiple_of(r * S, S), S)
        return pltpu.make_async_copy(x_h.at[rows], x.at[rows], x_sem.at[r])

    loads = [
        pltpu.make_async_copy(src, dst, load_sem.at[i])
        for i, (src, dst) in enumerate(
            (
                (va_h, va), (vb_h, vb), (qkv_h, qkv), (out_h, outw), (fin_h, fin), (fout_h, fout),
                (place_h, place),
            )
        )
    ]
    for copy in [loads[6]] + [x_load(r) for r in range(R)] + loads[:6]:
        copy.start()

    barrier = pltpu.get_barrier_semaphore()
    for d in range(1, G):
        pl.semaphore_signal(barrier, inc=1, device_id={"heads": lax.rem(z + d, G)}, device_id_type=MESH)
    for d in range(1, NR):
        pl.semaphore_signal(barrier, inc=1, device_id={"rows": lax.rem(rw + d, NR)}, device_id_type=MESH)
    pl.semaphore_wait(barrier, G - 1 + NR - 1)

    def over(axis, d, src, dst, send, recv):
        me, size = (z, G) if axis == "heads" else (rw, NR)
        return pltpu.make_async_remote_copy(
            src_ref=src, dst_ref=dst, send_sem=send, recv_sem=recv,
            device_id={axis: lax.rem(me + d, size)}, device_id_type=MESH,
        )

    lane = iota((1, LANES), 1)
    low_half = lane < HDIM
    jcol = iota((SEGS, 1), 0)
    slot = iota((1, S), 1)

    def expand(f):
        tiles = [jnp.where(low_half, f[:, 2 * t : 2 * t + 1], f[:, 2 * t + 1 : 2 * t + 2]) for t in range(PAIRS)]
        return jnp.concatenate(tiles, 1)

    def compress(v):
        out = jnp.zeros((v.shape[0], LANES), F32)
        for t in range(PAIRS):
            tile = v[:, LANES * t : LANES * (t + 1)]
            a = jnp.sum(jnp.where(low_half, tile, 0.0), -1, keepdims=True)
            b = jnp.sum(jnp.where(low_half, 0.0, tile), -1, keepdims=True)
            out = jnp.where(lane == 2 * t, a, jnp.where(lane == 2 * t + 1, b, out))
        return out

    e1 = [over("heads", d, lead_out, lead_in.at[d], e1_s.at[d], e1_r.at[d]) for d in range(1, G)]
    for copy in e1:
        copy.start()

    eye = iota((SEGS, SEGS), 0) == iota((SEGS, SEGS), 1)
    task_lane = lane & (TASKS - 1)
    counts = jnp.zeros((SEGS, LANES), F32)
    for r in range(R):
        seg_row = seg[r : r + 1, :]
        local = ids[r : r + 1, :] - z * V
        own = (local >= 0) & (local < V)
        first = (slot == 0) | (seg_row != pltpu.roll(seg_row, 1, 1))
        seg_eff[r : r + 1, :] = jnp.where(own & (first | (slot < fill[r])), seg_row, -1)
        starts = jnp.sum((seg_row < jcol).astype(jnp.int32), 1, keepdims=True)
        starts_s[r] = jnp.broadcast_to(starts, (SEGS, LANES))
        lead = (starts < fill[r]).astype(F32)
        task = jnp.sum(jnp.where(eye, tasks[r : r + 1, :], 0), 1, keepdims=True)
        counts = counts + jnp.where((task == task_lane) & (lane < TASKS * CLASSES), lead, 0.0)
    cnt_out[...] = counts
    cnt = [over("rows", d, cnt_out, cnt_in.at[d], cnt_ss.at[d], cnt_rs.at[d]) for d in range(1, NR)]
    for copy in cnt:
        copy.start()
    gain0, shift0 = gains[0:1, :], shifts[0:1, :]
    loads[6].wait()
    places[...] = place[2:, :]
    prow = iota((places.shape[0], 1), 0)

    def norm_row(r, _):
        seg_row = seg[pl.ds(r, 1), :]
        begin = jnp.sum(jnp.where(seg_row == jcol, starts_s[r][:, 0:1], 0), 0, keepdims=True)
        offset = slot - begin
        x_load(r).wait()
        for b in range(S // BLK):
            one = (prow == offset[:, b * BLK : (b + 1) * BLK]).astype(F32).astype(BF)
            rows = pl.ds(pl.multiple_of(r * S + b * BLK, BLK), BLK)
            hat, _ = normed(mm_l(one, places[...]) + x[rows, :].astype(F32))
            x[rows, :] = (hat * gain0 + shift0).astype(BF)
        return 0

    lax.fori_loop(0, R, norm_row, 0)

    for copy in e1:
        copy.wait()
    word = lead_out[...].astype(F32)
    for d in range(1, G):
        word = word + lead_in[d].astype(F32)
    hat, _ = normed(word + places[0:1, :].astype(F32))
    xz = hat * gain0 + shift0
    xz_s[...] = xz
    xl = xz.astype(BF)
    loads[0].wait()
    latent = mm(xl, va[...])
    latent_s[...] = latent
    loads[1].wait()
    eq_s[...] = mm((latent * scale_d[0:1, :]).astype(BF), vb[...])
    loads[2].wait()

    def tile_at(t):
        return pl.ds(pl.multiple_of(LANES * t, LANES), LANES)

    def absorb(t, _):
        r = mm(xl, qkv[:, pl.ds(pl.multiple_of(384 * t, LANES), 256)])
        at = tile_at(t)
        q = jnp.where(low_half, r[:, :LANES], r[:, LANES:]) + (biases[0:1, at] + scale_b[0:1, at] * eq_s[:, at])
        turned = pltpu.roll(q.astype(BF).astype(F32) * 0.125, HDIM, 1)
        a0 = mm_t(jnp.where(low_half, 0.0, turned).astype(BF), qkv[:, tile_at(3 * t)])
        a1 = mm_t(jnp.where(low_half, turned, 0.0).astype(BF), qkv[:, tile_at(3 * t + 2)])
        both = pl.ds(pl.multiple_of(16 * t, 16), 16)
        for r_ in range(R):
            rows = slice(r_ * SEGS, (r_ + 1) * SEGS)
            qk[r_, both, :] = jnp.concatenate([a0[rows], a1[rows]], 0).astype(BF)
        return 0

    lax.fori_loop(0, PAIRS, absorb, 0, unroll=UNROLL)

    Q = HEADS * SEGS
    qj = lax.rem(iota((Q, 1), 0), SEGS)
    hsub = iota((HEADS, SEGS, LANES), 0)
    hlane = iota((HEADS, SEGS, LANES), 2)

    def to_lanes(col):
        return jnp.sum(jnp.where(hsub == hlane, col.reshape(HEADS, SEGS, 1), 0.0), 0)

    def to_col(f):
        wide = jnp.broadcast_to(f[None], (HEADS, SEGS, LANES))
        return jnp.sum(jnp.where(hsub == hlane, wide, 0.0), -1, keepdims=True).reshape(Q, 1)

    def attend(p, _):
        parts = []
        for i in range(2):
            r = 2 * p + i
            xr = x[pl.ds(pl.multiple_of(r * S, S), S), :]
            mask = seg_eff[pl.ds(r, 1), :] == qj
            sc = jnp.where(mask, mm_t(qk[r], xr), NEG)
            top = jnp.max(sc, -1, keepdims=True)
            e = jnp.where(mask, jnp.exp(sc - top), 0.0)
            expo[r] = e
            st[r] = to_lanes(top) + pltpu.roll(to_lanes(jnp.sum(e, -1, keepdims=True)), HDIM, 1)
            parts.append(mm(e.astype(BF), xr).reshape(HEADS, SEGS, D))
        ub[:, pl.ds(pl.multiple_of(2 * SEGS * p, 2 * SEGS), 2 * SEGS), :] = jnp.concatenate(parts, 1).astype(BF)
        return 0

    lax.fori_loop(0, R // 2, attend, 0)

    def row_of(d):
        return lax.rem(lax.rem(z + d, G), R)

    rs = [over("heads", d, st.at[row_of(d)], st_in.at[d], rs_s.at[0, d], rs_r.at[0, d]) for d in range(1, G)]
    for copy in rs:
        copy.start()

    NT = 256

    def cols(n):
        return pl.ds(pl.multiple_of(NT * n, NT), NT)

    def latents(n, _):
        ua[:, cols(n)] = mm(ub[...].reshape(HEADS * L, D), va[:, cols(n)])
        return 0

    lax.fori_loop(0, D // NT, latents, 0, unroll=D // NT)

    def two(t):
        return pl.ds(pl.multiple_of(2 * L * t, 2 * L), 2 * L)

    def values(t, _):
        at = tile_at(t)
        v0 = mm(ub[2 * t], qkv[:, tile_at(3 * t + 1)])
        v1 = mm(ub[2 * t + 1], qkv[:, tile_at(3 * t + 2)])
        pair = mm((ua[two(t), :] * scale_d[1:2, :]).astype(BF), vb[:, at])
        extra = jnp.where(low_half, pair[:L], pair[L:])
        ev[:, at] = extra
        mixed = jnp.where(low_half, v0, v1) + scale_b[1:2, at] * extra
        pack[:, :, at] = mixed.reshape(R, SEGS, LANES)
        return 0

    for half in range(2):
        lax.fori_loop(half * PAIRS // 2, (half + 1) * PAIRS // 2, values, 0, unroll=PAIRS // 2)
        left, quarter = half * D // 2, D // 4
        for r in range(R):
            parts = [pack[r, :, left : left + quarter], pack[r, :, left + quarter : left + 2 * quarter]]
            pk[r, half] = jnp.concatenate(parts, 0).astype(BF)
        leg = [
            over("heads", d, pk.at[row_of(d), half], pk_in.at[d, half], rs_s.at[1 + half, d], rs_r.at[1 + half, d])
            for d in range(1, G)
        ]
        for copy in leg:
            copy.start()
        rs = rs + leg

    def widen(halves):
        both = [halves[i].astype(F32) for i in range(2)]
        return jnp.concatenate([v for h in both for v in (h[:SEGS], h[SEGS:])], 1)

    for copy in cnt:
        copy.wait()
    total = cnt_out[...]
    for d in range(1, NR):
        total = total + cnt_in[d]
    count = jnp.sum(total, 0, keepdims=True)
    weights = jnp.zeros((1, LANES), F32)
    for t in range(TASKS):
        weights = jnp.where(task_lane == t, task_w[t].astype(F32), weights)
    coef = weights / jnp.maximum(count, 1.0)
    task = jnp.sum(jnp.where(eye, tasks[pl.ds(own_r, 1), :], 0), 1, keepdims=True)
    label = jnp.sum(jnp.where(eye, labels[pl.ds(own_r, 1), :], 0), 1, keepdims=True)
    picked = (task == task_lane) & (lane < TASKS * CLASSES)
    target = picked & (lane // TASKS == label)
    leads = (starts_s[own_r][:, 0:1] < fill[own_r]) & (z < R)
    weight = jnp.sum(jnp.where(target, coef, 0.0), -1, keepdims=True)
    weight = jnp.where(leads, weight, 0.0)
    tab[...] = jnp.concatenate([table[...], jnp.zeros((LANES - TASKS * CLASSES, D), F32)], 0).astype(BF)

    for copy in rs:
        copy.wait()
    got = [pack[own_r]] + [widen(pk_in[d]) for d in range(1, G)]
    stat = [st[own_r]] + [st_in[d] for d in range(1, G)]
    top = stat[0]
    for part in stat[1:]:
        top = jnp.maximum(top, part)
    shrink = [jnp.exp(part - top) for part in stat]
    tot = jnp.zeros((SEGS, LANES), F32)
    for part, s in zip(stat, shrink):
        tot = tot + pltpu.roll(part, HDIM, 1) * s
    tot = jnp.where(lane < HEADS, tot, 1.0)
    lse_out[...] = top + jnp.log(tot)
    mixed = jnp.zeros((SEGS, D), F32)
    for part, s in zip(got, shrink):
        mixed = mixed + expand(s / tot) * part
    mixed = mixed + biases[1:2, :]

    def guarded(cond, f):
        if cond is None:
            f()
        else:
            pl.when(cond)(f)

    mine = None if G == R else z < R

    def hand_out(k, src, dst):
        def start():
            for d in range(1, G):
                over("heads", d, src, dst.at[own_r], g_s.at[k, d], g_r.at[k, own_r]).start()

        def keep():
            dst[own_r] = src[...]

        guarded(mine, start)
        guarded(mine, keep)

    def take_in(k, src, dst):
        def one(r):
            pltpu.make_async_remote_copy(
                src_ref=src, dst_ref=dst.at[r], send_sem=g_s.at[k, 0], recv_sem=g_r.at[k, r],
                device_id={"heads": z}, device_id_type=MESH,
            ).wait_recv()

        for r in range(R):
            pl.when(z != r)(functools.partial(one, r))

    hand_out(0, lse_out, lse_in)

    loads[3].wait()
    r_one = xz_s[pl.ds(pl.multiple_of(own_r * SEGS, SEGS), SEGS), :] + mm(mixed.astype(BF), outw[...]) + biases[2:3, :]
    hat1, rstd1 = normed(r_one)
    x_one = hat1 * gains[1:2, :] + shifts[1:2, :]
    x_one_low = x_one.astype(BF)
    loads[4].wait()

    for n in range(FF // FT):
        at = slice(FT * n, FT * (n + 1))
        act[:, at] = mm(x_one_low, fin[:, at])
    h = act[...] + bias_in[...]
    half = 0.5 * (1.0 + lax.erf(h * 0.7071067811865476))
    act[...] = h * half
    slope[...] = half + h * (0.3989422804014327 * jnp.exp(-0.5 * h * h))
    loads[5].wait()
    act_low = act[...].astype(BF)

    def ffn_out_tile(n, _):
        fx[0:SEGS, cols(n)] = mm(act_low, fout[:, cols(n)])
        return 0

    lax.fori_loop(0, D // NT, ffn_out_tile, 0, unroll=D // NT)
    hat2, rstd2 = normed(x_one + fx[0:SEGS, :] + biases[3:4, :])
    x_two = (hat2 * gains[2:3, :] + shifts[2:3, :]).astype(BF)
    logits = mm_t(x_two, tab[...])
    chosen = jnp.where(picked, logits, NEG)
    peak = jnp.max(chosen, -1, keepdims=True)
    sums = jnp.sum(jnp.where(picked, jnp.exp(chosen - peak), 0.0), -1, keepdims=True)
    log_sum = peak + jnp.log(sums)
    hit = jnp.sum(jnp.where(target, logits, 0.0), -1, keepdims=True)
    loss = jnp.sum(weight * (log_sum - hit), 0, keepdims=True)
    soft = jnp.where(picked, jnp.exp(chosen - log_sum), 0.0) - target.astype(F32)
    g_logits = (weight * soft).astype(BF)
    hs[...] = mm(g_logits.astype(F32).T.astype(BF), x_two)[: CHUNKS * 8, :]
    hs[TASKS * CLASSES : TASKS * CLASSES + 8, :] = jnp.broadcast_to(loss, (8, D))
    g_two = mm(g_logits, tab[...])
    g_r2 = norm_back(hat2, rstd2, gains[2:3, :], g_two)
    g_f = g_r2.astype(BF)

    for n in range(FF // FT):
        at = slice(FT * n, FT * (n + 1))
        gh[:, at] = mm_t(g_f, fout[at, :]) * slope[:, at]
    gh_low = gh[...].astype(BF)

    def back_in(n, _):
        fx[0:SEGS, cols(n)] = mm_t(gh_low, fin[cols(n), :])
        return 0

    lax.fori_loop(0, D // NT, back_in, 0, unroll=D // NT)
    g_r1 = norm_back(hat1, rstd1, gains[1:2, :], g_r2 + fx[0:SEGS, :])
    g_mixed = mm_t(g_r1.astype(BF), outw[...]).astype(BF).astype(F32)
    quarters = [g_mixed[:, i * D // 4 : (i + 1) * D // 4] for i in range(4)]
    gpk[0] = jnp.concatenate(quarters[0:2], 0).astype(BF)
    gpk[1] = jnp.concatenate(quarters[2:4], 0).astype(BF)
    hand_out(1, gpk, gpk_in)
    dlt_out[...] = compress(g_mixed * mixed) - compress(g_mixed * biases[1:2, :])
    hand_out(2, dlt_out, dlt_in)

    def spread(src, dst, send, recv, limit, action):
        for d in range(1, G):
            copy = over("heads", d, src(lax.rem(z + d, G)), dst(d), send.at[d], recv(d))
            cond = limit(lax.rem(z + d, G))
            if cond is None:
                action(copy)
            else:
                pl.when(cond)(functools.partial(action, copy))

    def chunk_of(peer):
        return hs.at[pl.ds(pl.multiple_of(8 * lax.rem(peer, CHUNKS), 8), 8)]

    def small(peer):
        return None if G == CHUNKS else peer < CHUNKS

    holder = None if G == CHUNKS else z < CHUNKS
    take_in(0, lse_out, lse_in)
    take_in(1, gpk, gpk_in)
    for r in range(R):
        g_in[r] = widen(gpk_in[r])

    scale = [jnp.exp(st[r] - lse_in[r]) for r in range(R)]
    factor = jnp.concatenate([jnp.where(lane < HEADS, s, 0.0) for s in scale], 0)

    def back_value(t, acc):
        at = tile_at(t)
        g = g_in[:, :, at].reshape(L, LANES)
        z0 = mm_t(jnp.where(low_half, g, 0.0).astype(BF), qkv[:, tile_at(3 * t + 1)])
        z1 = mm_t(jnp.where(low_half, 0.0, g).astype(BF), qkv[:, tile_at(3 * t + 2)])
        zacc[two(t), :] = jnp.concatenate([z0, z1], 0)
        gb = g * scale_b[1:2, at]
        both = jnp.concatenate([jnp.where(low_half, gb, 0.0), jnp.where(low_half, 0.0, gb)], 0).astype(BF)
        back = mm_t(both, vb[:, at])
        f0 = jnp.sum(jnp.where(lane == 2 * t, factor, 0.0), -1, keepdims=True)
        f1 = jnp.sum(jnp.where(lane == 2 * t + 1, factor, 0.0), -1, keepdims=True)
        acc = acc + jnp.sum(jnp.concatenate([f0, f1], 0) * ua[two(t), :] * back, 0, keepdims=True)
        zb[two(t), :] = (back * scale_d[1:2, :]).astype(BF)
        return acc

    grad_d1 = lax.fori_loop(0, PAIRS, back_value, jnp.zeros((1, D), F32), unroll=UNROLL)
    grad_b1 = jnp.sum(g_in[...].reshape(L, D) * ev[...] * expand(factor), 0, keepdims=True)
    extra = TASKS * CLASSES + 1
    hs[extra : extra + 2, :] = jnp.concatenate([grad_d1, grad_b1], 0)
    spread(chunk_of, lambda d: h_in.at[d], h_ss, lambda d: h_rs.at[d], small, lambda c: c.start())

    def back_latent(n, _):
        at = cols(n)
        part = (zacc[:, at] + mm_t(zb[...], va[at, :])).reshape(HEADS, R, SEGS, NT)
        for r in range(R):
            zq[r, :, at] = part[:, r].reshape(Q, NT).astype(BF)
        return 0

    lax.fori_loop(0, D // NT, back_latent, 0, unroll=D // NT)

    def relay():
        acc = chunk_of(z)[...]
        for d in range(1, G):
            over("heads", d, chunk_of(z), h_in.at[d], h_ss.at[d], h_rs.at[d]).wait_recv()
            acc = acc + h_in[d]
        hr[...] = acc
        for d in range(1, NR):
            over("rows", d, hr, hr_in.at[d], hr_ss.at[d], hr_rs.at[d]).start()

    def attend_back(p, _):
        parts = []
        for i in range(2):
            r = 2 * p + i
            xr = x[pl.ds(pl.multiple_of(r * S, S), S), :]
            f = to_col(jnp.where(lane < HEADS, jnp.exp(st[r] - lse_in[r]), 0.0))
            delta = to_col(dlt_in[r])
            ds = (expo[r] * f) * (mm_t(zq[r], xr) - delta)
            parts.append(mm(ds.astype(BF), xr).reshape(HEADS, SEGS, D))
        ub[:, pl.ds(pl.multiple_of(2 * SEGS * p, 2 * SEGS), 2 * SEGS), :] = jnp.concatenate(parts, 1).astype(BF)
        return 0

    take_in(2, dlt_out, dlt_in)
    lax.fori_loop(0, R // 4, attend_back, 0)
    guarded(holder, relay)
    lax.fori_loop(R // 4, R // 2, attend_back, 0)

    def relay_two():
        acc = hr[...]
        for d in range(1, NR):
            over("rows", d, hr, hr_in.at[d], hr_ss.at[d], hr_rs.at[d]).wait()
            acc = acc + hr_in[d]
        ag[lax.rem(z, CHUNKS)] = acc
        for d in range(1, G):
            c = lax.rem(z, CHUNKS)
            over("heads", d, ag.at[c], ag.at[c], ag_ss.at[d], ag_rs.at[c]).start()

    def back_query(t, _):
        at = tile_at(t)
        k0 = mm(ub[2 * t], qkv[:, tile_at(3 * t)])
        k1 = mm(ub[2 * t + 1], qkv[:, tile_at(3 * t + 2)])
        gq_s[:, at] = pltpu.roll(jnp.where(low_half, k1, k0), HDIM, 1) * 0.125
        return 0

    lax.fori_loop(0, PAIRS, back_query, 0, unroll=UNROLL)
    g_query = gq_s[...]
    grad_b0 = jnp.sum(g_query * eq_s[...], 0, keepdims=True)
    back = mm_t((g_query * scale_b[0:1, :]).astype(BF), vb[...])
    grad_d0 = jnp.sum(latent_s[...] * back, 0, keepdims=True)
    two_rows = jnp.concatenate([grad_d0, grad_b0], 0)
    late[...] = jnp.concatenate([two_rows[:, i * D // 4 : (i + 1) * D // 4] for i in range(4)], 0)
    leg = [over("heads", d, late, lz_in.at[d], lz_ss.at[d], lz_rs.at[d]) for d in range(1, G)]
    for copy in leg:
        copy.start()
    guarded(holder, relay_two)
    for copy in leg:
        copy.wait()
    acc = late[...]
    for d in range(1, G):
        acc = acc + lz_in[d]
    lr[...] = acc
    leg = [over("rows", d, lr, lr_in.at[d], lr_ss.at[d], lr_rs.at[d]) for d in range(1, NR)]
    for copy in leg:
        copy.start()

    for c in range(CHUNKS):
        def arrive(c=c):
            pltpu.make_async_remote_copy(
                src_ref=ag.at[c], dst_ref=ag.at[c], send_sem=ag_ss.at[0], recv_sem=ag_rs.at[c],
                device_id={"heads": z}, device_id_type=MESH,
            ).wait_recv()

        pl.when(z != c)(arrive)
    heads_sum[...] = ag[...].reshape(CHUNKS * 8, D)
    def handed():
        for k, (src, dst) in enumerate(((lse_out, lse_in), (gpk, gpk_in), (dlt_out, dlt_in))):
            for d in range(1, G):
                over("heads", d, src, dst.at[own_r], g_s.at[k, d], g_r.at[k, own_r]).wait_send()

    guarded(mine, handed)
    spread(chunk_of, lambda d: h_in.at[d], h_ss, lambda d: h_rs.at[d], small, lambda c: c.wait_send())

    def sent():
        for d in range(1, G):
            c = lax.rem(z, CHUNKS)
            over("heads", d, ag.at[c], ag.at[c], ag_ss.at[d], ag_rs.at[c]).wait_send()

    guarded(holder, sent)
    for copy in leg:
        copy.wait()
    acc = lr[...]
    for d in range(1, NR):
        acc = acc + lr_in[d]
    small_sum[...] = acc


def update_kernel(
    heads_sum, small_sum, scale_d, scale_b, table, mom_d, mom_b, mom_h, avg_d, avg_b, avg_h,
    loss, m_d, m_b, m_h, w_d, w_b, w_h, a_d, a_b, a_h, low, stats,
):
    count = table.shape[0]
    pairs = jnp.concatenate([small_sum[2 * i : 2 * i + 2, :] for i in range(4)], 1)
    more = heads_sum[count + 1 : count + 3, :]
    grad_d = jnp.concatenate([pairs[0:1], more[0:1]], 0)
    grad_b = jnp.concatenate([pairs[1:2], more[1:2]], 0)
    m_d[...], new_d, a_d[...] = update(scale_d[...], grad_d, mom_d[...], avg_d[...], RATE_D)
    m_b[...], new_b, a_b[...] = update(scale_b[...], grad_b, mom_b[...], avg_b[...], RATE_B)
    m_h[...], new_h, a_h[...] = update(table[...], heads_sum[:count, :], mom_h[...], avg_h[...], RATE_HEADS)
    w_d[...], w_b[...], w_h[...], low[...] = new_d, new_b, new_h, new_h.astype(BF)
    loss[...] = heads_sum[count : count + 1, 0:1]
    rms = [jnp.sqrt(jnp.mean(jnp.mean(v * v, 1, keepdims=True), 0, keepdims=True)) for v in (new_d, new_b)]
    stats[...] = jnp.concatenate(rms, 1)


def on_device(
    sizes,
    token_ids, segment_ids, row_fill, task_ids, labels, task_weights,
    word_table, position_table, norm_gains, norm_biases, dense_biases,
    qkv_weight, out_weight, ffn_in, ffn_bias, ffn_out, vera_a, vera_b,
    scale_d, scale_b, task_heads, mom_d, mom_b, mom_heads, avg_d, avg_b, avg_heads,
):
    G, NR = sizes
    R, S = token_ids.shape
    V, D = word_table.shape
    FF = ffn_in.shape[1]
    L, Q, T = R * SEGS, HEADS * SEGS, R * S
    raw, leads = gather(token_ids, segment_ids, row_fill, word_table)

    def flat(value):
        return value.transpose(1, 0, 2).reshape(CLASSES * TASKS, D)

    table, mom_h, avg_h = flat(task_heads), flat(mom_heads), flat(avg_heads)
    v = pltpu.VMEM
    dma = pltpu.SemaphoreType.DMA
    scratch = [
        v((T, D), BF), v(qkv_weight.shape, BF), v(out_weight.shape, BF), v(ffn_in.shape, BF), v(ffn_out.shape, BF),
        v(vera_a.shape, BF), v(vera_b.shape, BF),
        v(position_table.shape, BF), v((position_table.shape[0] - 2, D), BF), v((G, L, D), BF), v((R, S), jnp.int32), v((R, SEGS, LANES), jnp.int32), v((L, D), F32),
        v((L, D), F32), v((L, D), F32), v((R, Q, D), BF), v((R, Q, S), F32), v((HEADS, L, D), BF),
        v((HEADS * L, D), F32), v((L, D), F32), v((R, SEGS, D), F32), v((R, SEGS, LANES), F32), v((G, SEGS, LANES), F32),
        v((R, 2, 2 * SEGS, D // 4), BF), v((G, 2, 2 * SEGS, D // 4), BF),
        v((SEGS, FF), F32), v((SEGS, FF), F32), v((SEGS, FF), F32), v((LANES, D), BF), v((SEGS, LANES), F32), v((R, SEGS, LANES), F32),
        v((2, 2 * SEGS, D // 4), BF), v((R, 2, 2 * SEGS, D // 4), BF), v((SEGS, LANES), F32), v((R, SEGS, LANES), F32),
        v((R, SEGS, D), F32), v((R, Q, D), BF), v((HEADS * L, D), F32), v((HEADS * L, D), BF), v((L, D), F32),
        v((L, D), F32),
        v((SEGS, LANES), F32), v((NR, SEGS, LANES), F32), v((CHUNKS * 8, D), F32), v((G, 8, D), F32), v((8, D), F32),
        v((NR, 8, D), F32), v((CHUNKS, 8, D), F32), v((8, D // 4), F32), v((G, 8, D // 4), F32), v((8, D // 4), F32),
        v((NR, 8, D // 4), F32),
        dma((7,)), dma((R,)), dma((G,)), dma((G,)), dma((NR,)), dma((NR,)), dma((3, G)), dma((3, G)),
        dma((3, G)), dma((3, R)), dma((G,)), dma((G,)), dma((NR,)), dma((NR,)), dma((G,)), dma((CHUNKS,)),
        dma((G,)), dma((G,)), dma((NR,)), dma((NR,)),
    ]
    vm, hbm, sm = (pl.BlockSpec(memory_space=m) for m in (pltpu.VMEM, pl.ANY, pltpu.SMEM))
    heads_sum, small_sum = pl.pallas_call(
        functools.partial(step_kernel, (R, S, G, NR, V)),
        out_shape=(jax.ShapeDtypeStruct((CHUNKS * 8, D), F32), jax.ShapeDtypeStruct((8, D // 4), F32)),
        in_specs=[sm, sm] + [vm] * 12 + [hbm] * 8,
        out_specs=(vm, vm),
        scratch_shapes=scratch,
        compiler_params=pltpu.CompilerParams(
            collective_id=0, has_side_effects=True, vmem_limit_bytes=60 * 1024 * 1024
        ),
    )(
        row_fill, task_weights, token_ids, segment_ids, task_ids, labels, leads, norm_gains, norm_biases,
        dense_biases, ffn_bias.reshape(1, -1), scale_d, scale_b, table,
        raw, position_table, qkv_weight, out_weight, ffn_in, ffn_out, vera_a, vera_b,
    )
    like = jax.ShapeDtypeStruct
    two, many = like((2, D), F32), like((CLASSES * TASKS, D), F32)
    loss, m_d, m_b, m_h, w_d, w_b, w_h, a_d, a_b, a_h, low, stats = pl.pallas_call(
        update_kernel,
        out_shape=(
            like((1, 1), F32), two, two, many, two, two, many, two, two, many, like((CLASSES * TASKS, D), BF), like((1, 2), F32),
        ),
        in_specs=[vm] * 11,
        out_specs=(vm,) * 12,
    )(heads_sum, small_sum, scale_d, scale_b, table, mom_d, mom_b, mom_h, avg_d, avg_b, avg_h)

    def unflat(value):
        return value.reshape(CLASSES, TASKS, D).transpose(1, 0, 2)

    return (
        loss.reshape(()), m_d, m_b, unflat(m_h), w_d, w_b, unflat(w_h), a_d, a_b, unflat(a_h), unflat(low), stats.reshape(2),
    )


def solution(mesh):
    sizes = (mesh.shape["heads"], mesh.shape["rows"])
    by_row = P("rows", None)
    return jax.shard_map(
        functools.partial(on_device, sizes),
        mesh=mesh,
        in_specs=(by_row, by_row, P("rows"), by_row, by_row, P(), P("heads", None)) + (P(),) * 20,
        out_specs=(P(),) * 12,
        check_vma=False,
    )
```

profile of v0, /device:TPU:0, one launch (start us, length us, event | category | flops | bytes accessed | tf_op | source)
XLA Modules:
  0.0 88.6 jit_solution(6942307250567292388)
XLA Ops:
  0.6 18.1 %shard_map.346 = (bf16[4096,1024]{1,0:T(8,128)(2,1)}, bf16[32,1024]{1,0:T(8,128)(2,1)}) custom-call(s32[4]{0:T(128)} %fill.3, s32[4,1024]{1,0:T(4,128)} %ids.3, s32[4,1024]{1,0:T(4,128)} %seg.3, bf16[12568,1024]{1,0:T(8,128)(2,1)} %words.1), custom_call_target="tpu_custom_call" | custom-call | tf_op jit(solution)/shard_map/pallas_call | solution.py:223
  18.8 67.7 %shard_map.347 = (f32[32,1024]{1,0:T(8,128)}, f32[8,256]{1,0:T(8,128)}) custom-call(s32[4]{0:T(128)} %fill.3, s32[8]{0:T(128)} %task_w.1, s32[4,1024]{1,0:T(4,128)} %ids.3, s32[4,1024]{1,0:T(4,128)} %seg.3, s32[4,8]{1,0:T(4,128)} %tasks.1, s32[4,8]{1,0:T(4,128)} %labels.1, bf16[32,1024]{1,0:T(8,128)(2,1)} %get-tuple-element.28.lead_out, f32[3,1024]{1,0:T(4,128)} %gains.1, ...), custom_call_target="tpu_custom_call" | custom-call | tf_op jit(solution)/shard_map/pallas_call | solution.py:793
  86.5 1.9 %shard_map.348 = (f32[1,1]{1,0:T(1,128)}, f32[2,1024]{1,0:T(2,128)}, f32[2,1024]{1,0:T(2,128)}, f32[24,1024]{1,0:T(8,128)}, f32[2,1024]{1,0:T(2,128)}, /*index=5...) custom-call(f32[32,1024]{1,0:T(8,128)} %get-tuple-element.30.heads_s, ...), custom_call_target="tpu_custom_call" | custom-call | tf_op jit(solution)/shard_map/pallas_call | solution.py:809
where the time goes:
time: 88.5 us; the launch traced here: 88.6 us
  Pallas kernels  87.8 us (99%)
    pallas_call x1, Pallas kernels, on_device(): pl.pallas_call(functools.partial(step_kernel, (R, S, G, NR, V)), out_shap...  67.7 us
    pallas_call x1, Pallas kernels, gather(): pl.pallas_call(functools.partial(gather_kernel, (R, S, V)), out_shape=(ja...  18.1 us
    pallas_call x1, Pallas kernels, on_device(): pl.pallas_call(update_kernel, out_shape=(like((1, 1), F32), two, two, man...  1.94 us

commit v1 on v0

--- a/solution.py
+++ b/solution.py
@@ -19,6 +19,7 @@
 SUB = 2
 FT = 1024
 UNROLL = 8
+PART = 32
 EPSILON = 1e-05
 MOMENTUM = 0.9
 AVERAGE = 0.8
@@ -70,14 +71,14 @@
 
 def gather_kernel(
     cfg, fill, ids, seg, words, x_out, lead_out,
-    listv, lists, code, lead, list_sem, buf_sem, out_sem, *big,
+    listv, lists, code, lead, begins, bufs, stages, list_sem, buf_sem, out_sem,
 ):
     R, S, V = cfg
     D = x_out.shape[1]
     PER = S // BLK
     NB = R * PER
     HALVES = BLK // LANES
-    bufs, stages = big[:NB], big[NB:]
+    STAGES = stages.shape[0]
     z = lax.axis_index("heads")
     slot = iota((1, S), 1)
     lane = iota((1, LANES), 1)
@@ -96,11 +97,10 @@
     tiles = [need_f[:, LANES * k : LANES * (k + 1)] for k in range(S // LANES)]
     prefix = mm(jnp.concatenate(tiles, 0).astype(BF), upper)
     count_row = jnp.zeros((1, LANES), F32)
-    begins = []
     for r in range(R):
         seg_row = segs[r : r + 1, :]
         starts = jnp.sum((seg_row < jcol).astype(jnp.int32), 1, keepdims=True)
-        begins.append(starts)
+        begins[r] = jnp.broadcast_to(starts, (SEGS, LANES))
         for p in range(PER):
             b = r * PER + p
             here = slice(BLK * p, BLK * (p + 1))
@@ -117,7 +117,7 @@
             marks = jnp.where((rank // GROUP) == row8, iota((1, BLK), 1) + 1, 0).astype(F32).astype(BF)
             code[b] = mm_t(marks, spots)
             spots = (iota((LANES, 1), 0) == jnp.where(wanted, rank & (LANES - 1), -1)).astype(F32).astype(BF)
-            tile = word // SUB
+            tile = word // SUB * SUB
             plane = jnp.where(row8 < HALVES, tile & 255, tile // 256)
             plane = jnp.where(((rank // LANES) == (row8 & (HALVES - 1))) & (row8 < 2 * HALVES), plane, 0)
             both = mm_t(plane.astype(F32).astype(BF), spots)
@@ -129,7 +129,7 @@
     to_scalar.start()
     lead[...] = jnp.zeros_like(lead)
     for b in range(NB):
-        bufs[b][0 : GROUP * SUB // 8] = jnp.zeros((GROUP * SUB // 8, 8, D), BF)
+        bufs[b, 0 : GROUP * SUB // 8] = jnp.zeros((GROUP * SUB // 8, 8, D), BF)
     to_scalar.wait()
 
     def eights(b):
@@ -144,8 +144,8 @@
                 for u in range(8):
                     word = lists[HALVES * b + h, i * 8 + u]
                     pltpu.make_async_copy(
-                        words.at[pl.ds(pl.multiple_of(SUB * word, SUB), SUB)],
-                        bufs[b].at[h * GROUP * SUB // 8 + i * SUB + u * SUB // 8, pl.ds(u * SUB % 8, SUB)],
+                        words.at[pl.ds(pl.multiple_of(word, SUB), SUB)],
+                        bufs.at[b, h * GROUP * SUB // 8 + i * SUB + u * SUB // 8, pl.ds(u * SUB % 8, SUB)],
                         buf_sem.at[r],
                     ).start()
                 return 0
@@ -160,7 +160,7 @@
         total = eights(r * PER)
         for p in range(1, PER):
             total = total + eights(r * PER + p)
-        part = bufs[r * PER].at[pl.ds(0, SUB)]
+        part = bufs.at[0, pl.ds(0, SUB)]
 
         def eight(i, _):
             pltpu.make_async_copy(part, part, buf_sem.at[r]).wait()
@@ -171,43 +171,51 @@
     col = iota((BLK, 1), 0) + 1
 
     def pick(b, g):
-        spot = begins[b // PER] - BLK * (b % PER) + 1
+        spot = begins[b // PER][:, 0:1] - BLK * lax.rem(b, PER) + 1
         spot = jnp.where((spot >= 1) & (spot <= BLK), spot, -5)
         want = jnp.concatenate([col, spot, jnp.full((8, 1), -5, jnp.int32)], 0).astype(F32)
         one = (want == code[b, pl.ds(g, 1), :]).astype(F32).astype(BF)
-        rows = bufs[b][g * GROUP * SUB // 8 : (g + 1) * GROUP * SUB // 8]
+        rows = bufs[b, g * GROUP * SUB // 8 : (g + 1) * GROUP * SUB // 8]
         return mm(one, rows.reshape(GROUP * SUB, D))
 
     def add_lead(b, got):
-        rows = slice(b // PER * SEGS, (b // PER + 1) * SEGS)
+        rows = pl.ds(pl.multiple_of(b // PER * SEGS, SEGS), SEGS)
         lead[rows, :] = lead[rows, :] + got
 
     def out_copy(b):
-        return pltpu.make_async_copy(stages[b % (2 * PER)], x_out.at[pl.ds(b * BLK, BLK)], out_sem.at[b])
-
-    issue(0)
+        k = lax.rem(b, STAGES)
+        rows = pl.ds(pl.multiple_of(b * BLK, BLK), BLK)
+        return pltpu.make_async_copy(stages.at[k], x_out.at[rows], out_sem.at[k])
+
     for r in range(R):
-        if r + 1 < R:
-            issue(r + 1)
+        issue(r)
+
+    def row(r, _):
         arrive(r)
-        for b in range(r * PER, (r + 1) * PER):
-            if b >= 2 * PER:
-                out_copy(b - 2 * PER).wait()
+
+        def block(p, _):
+            b = r * PER + p
+            k = lax.rem(b, STAGES)
+            pl.when(b >= STAGES)(lambda: out_copy(b - STAGES).wait())
             got = pick(b, 0)
-            stages[b % (2 * PER)][...] = got[:BLK].astype(BF)
+            stages[k] = got[:BLK].astype(BF)
             add_lead(b, got[BLK : BLK + SEGS])
 
             @pl.when(lists[HALVES * NB, b] > GROUP)
-            def more(b=b):
+            def more():
                 got = pick(b, 1)
-                stages[b % (2 * PER)][...] = stages[b % (2 * PER)][...] + got[:BLK].astype(BF)
+                stages[k] = stages[k] + got[:BLK].astype(BF)
                 add_lead(b, got[BLK : BLK + SEGS])
 
             out_copy(b).start()
-
+            return 0
+
+        return lax.fori_loop(0, PER, block, 0)
+
+    lax.fori_loop(0, R, row, 0)
     lead_out[...] = lead[...].astype(BF)
-    for b in range(max(NB - 2 * PER, 0), NB):
-        out_copy(b).wait()
+    for k in range(STAGES):
+        out_copy(NB - STAGES + k).wait()
 
 
 def gather(token_ids, segment_ids, row_fill, word_table):
@@ -228,8 +236,8 @@
         scratch_shapes=[
             v((HALVES * NB + 8, LANES), jnp.int32),
             pltpu.SMEM((HALVES * NB + 8, LANES), jnp.int32), v((NB, 8, GROUP * SUB), F32),
-            v((R * SEGS, D), F32), dma((1,)), dma((R,)), dma((NB,)),
-            *[v((BLK * SUB // 8, 8, D), BF)] * NB, *[v((BLK, D), BF)] * (2 * PER),
+            v((R * SEGS, D), F32), v((R, SEGS, LANES), jnp.int32),
+            v((NB, BLK * SUB // 8, 8, D), BF), v((4, BLK, D), BF), dma((1,)), dma((R,)), dma((4,)),
         ],
         compiler_params=pltpu.CompilerParams(vmem_limit_bytes=60 * 1024 * 1024),
     )(row_fill, token_ids, segment_ids, word_table)
@@ -241,13 +249,14 @@
     x_h, place_h, qkv_h, out_h, fin_h, fout_h, va_h, vb_h,
     heads_sum, small_sum,
     x, qkv, outw, fin, fout, va, vb,
-    place, places, lead_in, seg_eff, starts_s, xz_s, latent_s, eq_s, qk, expo, ub, ua, ev, pack, st, st_in, pk, pk_in,
+    place, places, lead_in, seg_eff, starts_s, xz_s, latent_s, eq_s, qk, ub, ua, ev, pack, st, st_in, pk, pk_in,
     act, slope, gh, tab, lse_out, lse_in, gpk, gpk_in, dlt_out, dlt_in, g_in, zq, zacc, zb, gq_s, fx,
     cnt_out, cnt_in, hs, h_in, hr, hr_in, ag, late, lz_in, lr, lr_in,
     load_sem, x_sem, e1_s, e1_r, cnt_ss, cnt_rs, rs_s, rs_r, g_s, g_r, h_ss, h_rs, hr_ss, hr_rs, ag_ss, ag_rs,
-    lz_ss, lz_rs, lr_ss, lr_rs,
+    lz_ss, lz_rs, lr_ss, lr_rs, *wide,
 ):
     R, S, G, NR, V = cfg
+    expo, gdot, low, words = wide[:R], wide[R : R + 2], wide[R + 2 : 2 * R + 2], wide[2 * R + 2 :]
     D = x.shape[1]
     FF = fin.shape[1]
     PAIRS = HEADS // 2
@@ -256,9 +265,8 @@
     rw = lax.axis_index("rows")
     own_r = lax.rem(z, R)
 
-    def x_load(r):
-        rows = pl.ds(pl.multiple_of(r * S, S), S)
-        return pltpu.make_async_copy(x_h.at[rows], x.at[rows], x_sem.at[r])
+    def x_load(r, h):
+        return pltpu.make_async_copy(x_h.at[pl.ds(pl.multiple_of(r * S, S), S)], words[h], x_sem.at[h])
 
     loads = [
         pltpu.make_async_copy(src, dst, load_sem.at[i])
@@ -269,7 +277,7 @@
             )
         )
     ]
-    for copy in [loads[6]] + [x_load(r) for r in range(R)] + loads[:6]:
+    for copy in [x_load(0, 0), loads[6], x_load(1, 1)]:
         copy.start()
 
     barrier = pltpu.get_barrier_semaphore()
@@ -331,19 +339,38 @@
     places[...] = place[2:, :]
     prow = iota((places.shape[0], 1), 0)
 
-    def norm_row(r, _):
+    STEP = expo[0].shape[0]
+    blocks = S // STEP
+
+    def norm_row(r, h):
         seg_row = seg[pl.ds(r, 1), :]
         begin = jnp.sum(jnp.where(seg_row == jcol, starts_s[r][:, 0:1], 0), 0, keepdims=True)
         offset = slot - begin
-        x_load(r).wait()
-        for b in range(S // BLK):
-            one = (prow == offset[:, b * BLK : (b + 1) * BLK]).astype(F32).astype(BF)
-            rows = pl.ds(pl.multiple_of(r * S + b * BLK, BLK), BLK)
-            hat, _ = normed(mm_l(one, places[...]) + x[rows, :].astype(F32))
-            x[rows, :] = (hat * gain0 + shift0).astype(BF)
+        x_load(r, h).wait()
+
+        def place_rows(b):
+            one = (prow == offset[:, b * STEP : (b + 1) * STEP]).astype(F32).astype(BF)
+            expo[b % R][...] = mm_l(one, places[...])
+
+        place_rows(0)
+        for b in range(blocks):
+            if b + 1 < blocks:
+                place_rows(b + 1)
+            for c in range(0, STEP, PART):
+                at = b * STEP + c
+                hat, _ = normed(expo[b % R][c : c + PART, :] + words[h][at : at + PART, :].astype(F32))
+                x[pl.ds(pl.multiple_of(r * S + at, PART), PART), :] = (hat * gain0 + shift0).astype(BF)
+
+    def norm_two(i, _):
+        for h in range(2):
+            norm_row(2 * i + h, h)
+            pl.when(i + 1 < R // 2)(lambda h=h: x_load(2 * i + 2 + h, h).start())
         return 0
 
-    lax.fori_loop(0, R, norm_row, 0)
+    loads[0].start()
+    loads[1].start()
+    loads[2].start()
+    lax.fori_loop(0, R // 2, norm_two, 0)
 
     for copy in e1:
         copy.wait()
@@ -360,6 +387,8 @@
     loads[1].wait()
     eq_s[...] = mm((latent * scale_d[0:1, :]).astype(BF), vb[...])
     loads[2].wait()
+    for copy in loads[3:6]:
+        copy.start()
 
     def tile_at(t):
         return pl.ds(pl.multiple_of(LANES * t, LANES), LANES)
@@ -391,22 +420,44 @@
         wide = jnp.broadcast_to(f[None], (HEADS, SEGS, LANES))
         return jnp.sum(jnp.where(hsub == hlane, wide, 0.0), -1, keepdims=True).reshape(Q, 1)
 
-    def attend(p, _):
-        parts = []
-        for i in range(2):
-            r = 2 * p + i
-            xr = x[pl.ds(pl.multiple_of(r * S, S), S), :]
-            mask = seg_eff[pl.ds(r, 1), :] == qj
-            sc = jnp.where(mask, mm_t(qk[r], xr), NEG)
+    def rows_of(r):
+        return x[r * S : (r + 1) * S, :]
+
+    def score(r):
+        expo[r][...] = mm_t(qk[r], rows_of(r))
+
+    def soften(r):
+        tops, sums = [], []
+        for c in range(0, Q, PART):
+            rows = slice(c, c + PART)
+            mask = seg_eff[r : r + 1, :] == qj[rows]
+            sc = jnp.where(mask, expo[r][rows, :], NEG)
             top = jnp.max(sc, -1, keepdims=True)
             e = jnp.where(mask, jnp.exp(sc - top), 0.0)
-            expo[r] = e
-            st[r] = to_lanes(top) + pltpu.roll(to_lanes(jnp.sum(e, -1, keepdims=True)), HDIM, 1)
-            parts.append(mm(e.astype(BF), xr).reshape(HEADS, SEGS, D))
-        ub[:, pl.ds(pl.multiple_of(2 * SEGS * p, 2 * SEGS), 2 * SEGS), :] = jnp.concatenate(parts, 1).astype(BF)
-        return 0
-
-    lax.fori_loop(0, R // 2, attend, 0)
+            expo[r][rows, :] = e
+            low[r][rows, :] = e.astype(BF)
+            tops.append(top)
+            sums.append(jnp.sum(e, -1, keepdims=True))
+        top, total = jnp.concatenate(tops, 0), jnp.concatenate(sums, 0)
+        st[r] = to_lanes(top) + pltpu.roll(to_lanes(total), HDIM, 1)
+
+    def mix(r):
+        return mm(low[r][...], rows_of(r)).reshape(HEADS, SEGS, D)
+
+    def staged(first_part, second_part, between):
+        first_part(0)
+        held = None
+        for r in range(R):
+            if r + 1 < R:
+                first_part(r + 1)
+            second_part(r)
+            part = mix(r)
+            if r % 2:
+                ub[:, SEGS * (r - 1) : SEGS * (r + 1), :] = jnp.concatenate([held, part], 1).astype(BF)
+            held = part
+            between(r)
+
+    staged(score, soften, lambda r: None)
 
     def row_of(d):
         return lax.rem(lax.rem(z + d, G), R)
@@ -647,22 +698,19 @@
         for d in range(1, NR):
             over("rows", d, hr, hr_in.at[d], hr_ss.at[d], hr_rs.at[d]).start()
 
-    def attend_back(p, _):
-        parts = []
-        for i in range(2):
-            r = 2 * p + i
-            xr = x[pl.ds(pl.multiple_of(r * S, S), S), :]
-            f = to_col(jnp.where(lane < HEADS, jnp.exp(st[r] - lse_in[r]), 0.0))
-            delta = to_col(dlt_in[r])
-            ds = (expo[r] * f) * (mm_t(zq[r], xr) - delta)
-            parts.append(mm(ds.astype(BF), xr).reshape(HEADS, SEGS, D))
-        ub[:, pl.ds(pl.multiple_of(2 * SEGS * p, 2 * SEGS), 2 * SEGS), :] = jnp.concatenate(parts, 1).astype(BF)
-        return 0
+    def slope_of(r):
+        gdot[r % 2][...] = mm_t(zq[r], rows_of(r))
+
+    def bend(r):
+        f = to_col(jnp.where(lane < HEADS, jnp.exp(st[r] - lse_in[r]), 0.0))
+        delta = to_col(dlt_in[r])
+        for c in range(0, Q, PART):
+            rows = slice(c, c + PART)
+            ds = (expo[r][rows, :] * f[rows]) * (gdot[r % 2][rows, :] - delta[rows])
+            low[r][rows, :] = ds.astype(BF)
 
     take_in(2, dlt_out, dlt_in)
-    lax.fori_loop(0, R // 4, attend_back, 0)
-    guarded(holder, relay)
-    lax.fori_loop(R // 4, R // 2, attend_back, 0)
+    staged(slope_of, bend, lambda r: guarded(holder, relay) if r == R // 2 - 1 else None)
 
     def relay_two():
         acc = hr[...]
@@ -775,7 +823,7 @@
         v((T, D), BF), v(qkv_weight.shape, BF), v(out_weight.shape, BF), v(ffn_in.shape, BF), v(ffn_out.shape, BF),
         v(vera_a.shape, BF), v(vera_b.shape, BF),
         v(position_table.shape, BF), v((position_table.shape[0] - 2, D), BF), v((G, L, D), BF), v((R, S), jnp.int32), v((R, SEGS, LANES), jnp.int32), v((L, D), F32),
-        v((L, D), F32), v((L, D), F32), v((R, Q, D), BF), v((R, Q, S), F32), v((HEADS, L, D), BF),
+        v((L, D), F32), v((L, D), F32), v((R, Q, D), BF), v((HEADS, L, D), BF),
         v((HEADS * L, D), F32), v((L, D), F32), v((R, SEGS, D), F32), v((R, SEGS, LANES), F32), v((G, SEGS, LANES), F32),
         v((R, 2, 2 * SEGS, D // 4), BF), v((G, 2, 2 * SEGS, D // 4), BF),
         v((SEGS, FF), F32), v((SEGS, FF), F32), v((SEGS, FF), F32), v((LANES, D), BF), v((SEGS, LANES), F32), v((R, SEGS, LANES), F32),
@@ -785,9 +833,10 @@
         v((SEGS, LANES), F32), v((NR, SEGS, LANES), F32), v((CHUNKS * 8, D), F32), v((G, 8, D), F32), v((8, D), F32),
         v((NR, 8, D), F32), v((CHUNKS, 8, D), F32), v((8, D // 4), F32), v((G, 8, D // 4), F32), v((8, D // 4), F32),
         v((NR, 8, D // 4), F32),
-        dma((7,)), dma((R,)), dma((G,)), dma((G,)), dma((NR,)), dma((NR,)), dma((3, G)), dma((3, G)),
+        dma((7,)), dma((2,)), dma((G,)), dma((G,)), dma((NR,)), dma((NR,)), dma((3, G)), dma((3, G)),
         dma((3, G)), dma((3, R)), dma((G,)), dma((G,)), dma((NR,)), dma((NR,)), dma((G,)), dma((CHUNKS,)),
-        dma((G,)), dma((G,)), dma((NR,)), dma((NR,)),
+        dma((G,)), dma((G,)), dma((NR,)), dma((NR,)), *[v((Q, S), F32)] * (R + 2), *[v((Q, S), BF)] * R,
+        v((S, D), BF), v((S, D), BF),
     ]
     vm, hbm, sm = (pl.BlockSpec(memory_space=m) for m in (pltpu.VMEM, pl.ANY, pltpu.SMEM))
     heads_sum, small_sum = pl.pallas_call(

time: 88.5 us -> 86.1 us (0.973); the launches traced: 88.6 us -> 85.2 us
  Pallas kernels: 87.8 us -> 84.3 us
    pallas_call x1, Pallas kernels: 18.1 us -> 16.2 us  [gather(): pl.pallas_call(functools.partial(gather_kernel, (R, S, V)), out_shape=(ja...]
    pallas_call x1, Pallas kernels: 67.7 us -> 66.2 us  [on_device(): pl.pallas_call(functools.partial(step_kernel, (R, S, G, NR, V)), out_shap...]
where the time goes in v1:
time: 86.1 us; the launch traced here: 85.2 us
  Pallas kernels  84.3 us (98%)
    pallas_call x1, Pallas kernels, on_device(): pl.pallas_call(functools.partial(step_kernel, (R, S, G, NR, V)), out_shap...  66.2 us
    pallas_call x1, Pallas kernels, gather(): pl.pallas_call(functools.partial(gather_kernel, (R, S, V)), out_shape=(ja...  16.2 us
    pallas_call x1, Pallas kernels, on_device(): pl.pallas_call(update_kernel, out_shape=(like((1, 1), F32), two, two, man...  1.94 us

profile of v1, /device:TPU:0, one launch (start us, length us, event | category | flops | bytes accessed | tf_op | source)
XLA Modules:
  0.0 85.2 jit_solution(18056471388646367480)
XLA Ops:
  0.6 16.2 %shard_map.346 = (bf16[4096,1024]{1,0:T(8,128)(2,1)}, bf16[32,1024]{1,0:T(8,128)(2,1)}) custom-call(s32[4]{0:T(128)} %fill.3, s32[4,1024]{1,0:T(4,128)} %ids.3, s32[4,1024]{1,0:T(4,128)} %seg.3, bf16[12568,1024]{1,0:T(8,128)(2,1)} %words.1), custom_call_target="tpu_custom_call" | custom-call | tf_op jit(solution)/shard_map/pallas_call | solution.py:231
  16.9 66.2 %shard_map.347 = (f32[32,1024]{1,0:T(8,128)}, f32[8,256]{1,0:T(8,128)}) custom-call(s32[4]{0:T(128)} %fill.3, s32[8]{0:T(128)} %task_w.1, s32[4,1024]{1,0:T(4,128)} %ids.3, s32[4,1024]{1,0:T(4,128)} %seg.3, s32[4,8]{1,0:T(4,128)} %tasks.1, s32[4,8]{1,0:T(4,128)} %labels.1, bf16[32,1024]{1,0:T(8,128)(2,1)} %get-tuple-element.28.lead_out, f32[3,1024]{1,0:T(4,128)} %gains.1, ...), custom_call_target="tpu_custom_call" | custom-call | tf_op jit(solution)/shard_map/pallas_call | solution.py:842
  83.1 1.9 %shard_map.348 = (f32[1,1]{1,0:T(1,128)}, f32[2,1024]{1,0:T(2,128)}, f32[2,1024]{1,0:T(2,128)}, f32[24,1024]{1,0:T(8,128)}, f32[2,1024]{1,0:T(2,128)}, /*index=5...) custom-call(f32[32,1024]{1,0:T(8,128)} %get-tuple-element.30.heads_s, ...), custom_call_target="tpu_custom_call" | custom-call | tf_op jit(solution)/shard_map/pallas_call | solution.py:858

commit v2 on v1

--- a/solution.py
+++ b/solution.py
@@ -71,7 +71,7 @@
 
 def gather_kernel(
     cfg, fill, ids, seg, words, x_out, lead_out,
-    listv, lists, code, lead, begins, bufs, stages, list_sem, buf_sem, out_sem,
+    listv, lists, keyc, lead, bufs, stages, list_sem, buf_sem, out_sem,
 ):
     R, S, V = cfg
     D = x_out.shape[1]
@@ -92,38 +92,51 @@
         fills = jnp.where(iota((R, 1), 0) == r, fill[r], fills)
     first = (slot == 0) | (segs != pltpu.roll(segs, 1, 1))
     need = (local >= 0) & (local < V) & (first | (slot < fills))
-    need_f = need.astype(F32)
     upper = (iota((LANES, LANES), 0) <= iota((LANES, LANES), 1)).astype(F32).astype(BF)
-    tiles = [need_f[:, LANES * k : LANES * (k + 1)] for k in range(S // LANES)]
-    prefix = mm(jnp.concatenate(tiles, 0).astype(BF), upper)
+    ahead = iota((BLK, BLK), 0) < iota((BLK, BLK), 1)
+
+    def by_block(value):
+        return jnp.concatenate([value[:, BLK * p : BLK * (p + 1)] for p in range(PER)], 0)
+
+    pair = by_block(jnp.where(need, local // SUB, -1).astype(F32))
+    half = by_block((local & (SUB - 1)).astype(F32))
+    wanted = pair >= 0.0
+    pair_col = pair.T
+    same = [pair_col[:, q : q + 1] == pair[q : q + 1] for q in range(NB)]
+    seen = [jnp.max(jnp.where(same[q] & ahead, 1.0, 0.0), 0, keepdims=True) for q in range(NB)]
+    lead_one = jnp.where(wanted, 1.0 - jnp.concatenate(seen, 0), 0.0)
+    halves = [lead_one[:, LANES * h : LANES * (h + 1)] for h in range(HALVES)]
+    prefix = mm(jnp.concatenate(halves, 0).astype(BF), upper)
+    runs, total = [], jnp.zeros((NB, 1), F32)
+    for h in range(HALVES):
+        run = prefix[NB * h : NB * (h + 1)]
+        runs.append(run + total)
+        total = total + run[:, LANES - 1 :]
+    rank = jnp.where(lead_one > 0.0, jnp.concatenate(runs, 1) - 1.0, -1.0)
+    held = jnp.maximum(rank, 0.0)
     count_row = jnp.zeros((1, LANES), F32)
+    keys = []
+    for q in range(NB):
+        share = mm(jnp.broadcast_to(held[q : q + 1], (8, BLK)).astype(BF), same[q].astype(F32).astype(BF))
+        keys.append(share[0:1])
+    key = jnp.where(wanted, SUB * jnp.concatenate(keys, 0) + half, -1.0)
+    key_col = key.T
     for r in range(R):
-        seg_row = segs[r : r + 1, :]
-        starts = jnp.sum((seg_row < jcol).astype(jnp.int32), 1, keepdims=True)
-        begins[r] = jnp.broadcast_to(starts, (SEGS, LANES))
+        starts = jnp.sum((segs[r : r + 1, :] < jcol).astype(jnp.int32), 1, keepdims=True)
         for p in range(PER):
-            b = r * PER + p
-            here = slice(BLK * p, BLK * (p + 1))
-            runs, total = [], jnp.zeros((1, 1), F32)
-            for h in range(HALVES):
-                at = (HALVES * p + h) * R + r
-                runs.append(prefix[at : at + 1] + total)
-                total = total + prefix[at : at + 1, LANES - 1 :]
-            wanted = need_f[r : r + 1, here] > 0.0
-            rank = jnp.where(wanted, jnp.concatenate(runs, 1).astype(jnp.int32) - 1, -1)
-            word = local[r : r + 1, here]
-            key = jnp.where(wanted, (rank & (GROUP - 1)) * SUB + (word & (SUB - 1)), -1)
-            spots = (iota((GROUP * SUB, 1), 0) == key).astype(F32).astype(BF)
-            marks = jnp.where((rank // GROUP) == row8, iota((1, BLK), 1) + 1, 0).astype(F32).astype(BF)
-            code[b] = mm_t(marks, spots)
-            spots = (iota((LANES, 1), 0) == jnp.where(wanted, rank & (LANES - 1), -1)).astype(F32).astype(BF)
-            tile = word // SUB * SUB
-            plane = jnp.where(row8 < HALVES, tile & 255, tile // 256)
-            plane = jnp.where(((rank // LANES) == (row8 & (HALVES - 1))) & (row8 < 2 * HALVES), plane, 0)
+            b, q = r * PER + p, p * R + r
+            at_start = iota((1, BLK), 1) + BLK * p == starts
+            lead_key = jnp.sum(jnp.where(at_start, key[q : q + 1] + 8.0, 0.0), 1, keepdims=True) - 8.0
+            keyc[b] = jnp.concatenate([key_col[:, q : q + 1], lead_key, jnp.full((8, 1), -5.0, F32)], 0)
+            order = rank[q : q + 1].astype(jnp.int32)
+            spots = (iota((LANES, 1), 0) == jnp.where(order < 0, -1, order & (LANES - 1))).astype(F32).astype(BF)
+            row_at = SUB * pair[q : q + 1].astype(jnp.int32)
+            plane = jnp.where(row8 < HALVES, row_at & 255, row_at // 256)
+            plane = jnp.where(((order // LANES) == (row8 & (HALVES - 1))) & (row8 < 2 * HALVES), plane, 0)
             both = mm_t(plane.astype(F32).astype(BF), spots)
             both = both[0:HALVES] + 256.0 * both[HALVES : 2 * HALVES]
             listv[HALVES * b : HALVES * (b + 1), :] = both.astype(jnp.int32)
-            count_row = jnp.where(lane == b, total, count_row)
+            count_row = jnp.where(lane == b, total[q : q + 1], count_row)
     listv[HALVES * NB :, :] = jnp.broadcast_to(count_row.astype(jnp.int32), (8, LANES))
     to_scalar = pltpu.make_async_copy(listv, lists, list_sem.at[0])
     to_scalar.start()
@@ -168,13 +181,10 @@
 
         lax.fori_loop(0, total, eight, 0)
 
-    col = iota((BLK, 1), 0) + 1
+    lanes = iota((1, GROUP * SUB), 1).astype(F32)
 
     def pick(b, g):
-        spot = begins[b // PER][:, 0:1] - BLK * lax.rem(b, PER) + 1
-        spot = jnp.where((spot >= 1) & (spot <= BLK), spot, -5)
-        want = jnp.concatenate([col, spot, jnp.full((8, 1), -5, jnp.int32)], 0).astype(F32)
-        one = (want == code[b, pl.ds(g, 1), :]).astype(F32).astype(BF)
+        one = (keyc[b] == lanes + float(g * GROUP * SUB)).astype(F32).astype(BF)
         rows = bufs[b, g * GROUP * SUB // 8 : (g + 1) * GROUP * SUB // 8]
         return mm(one, rows.reshape(GROUP * SUB, D))
 
@@ -235,8 +245,8 @@
         out_specs=(hbm, vm),
         scratch_shapes=[
             v((HALVES * NB + 8, LANES), jnp.int32),
-            pltpu.SMEM((HALVES * NB + 8, LANES), jnp.int32), v((NB, 8, GROUP * SUB), F32),
-            v((R * SEGS, D), F32), v((R, SEGS, LANES), jnp.int32),
+            pltpu.SMEM((HALVES * NB + 8, LANES), jnp.int32), v((NB, BLK + 2 * SEGS, 1), F32),
+            v((R * SEGS, D), F32),
             v((NB, BLK * SUB // 8, 8, D), BF), v((4, BLK, D), BF), dma((1,)), dma((R,)), dma((4,)),
         ],
         compiler_params=pltpu.CompilerParams(vmem_limit_bytes=60 * 1024 * 1024),
@@ -610,8 +620,6 @@
     loss = jnp.sum(weight * (log_sum - hit), 0, keepdims=True)
     soft = jnp.where(picked, jnp.exp(chosen - log_sum), 0.0) - target.astype(F32)
     g_logits = (weight * soft).astype(BF)
-    hs[...] = mm(g_logits.astype(F32).T.astype(BF), x_two)[: CHUNKS * 8, :]
-    hs[TASKS * CLASSES : TASKS * CLASSES + 8, :] = jnp.broadcast_to(loss, (8, D))
     g_two = mm(g_logits, tab[...])
     g_r2 = norm_back(hat2, rstd2, gains[2:3, :], g_two)
     g_f = g_r2.astype(BF)
@@ -634,6 +642,8 @@
     hand_out(1, gpk, gpk_in)
     dlt_out[...] = compress(g_mixed * mixed) - compress(g_mixed * biases[1:2, :])
     hand_out(2, dlt_out, dlt_in)
+    hs[...] = mm(g_logits.astype(F32).T.astype(BF), x_two)[: CHUNKS * 8, :]
+    hs[TASKS * CLASSES : TASKS * CLASSES + 8, :] = jnp.broadcast_to(loss, (8, D))
 
     def spread(src, dst, send, recv, limit, action):
         for d in range(1, G):

time: 86.1 us -> 83.6 us (0.971)
  Pallas kernels: 84.3 us -> 82.4 us
    pallas_call x1, Pallas kernels: 66.2 us -> 64.5 us  [on_device(): pl.pallas_call(functools.partial(step_kernel, (R, S, G, NR, V)), out_shap...]
where the time goes in v2:
time: 83.6 us; the launch traced here: 83.2 us
  Pallas kernels  82.4 us (99%)
    pallas_call x1, Pallas kernels, on_device(): pl.pallas_call(functools.partial(step_kernel, (R, S, G, NR, V)), out_shap...  64.5 us
    pallas_call x1, Pallas kernels, gather(): pl.pallas_call(functools.partial(gather_kernel, (R, S, V)), out_shape=(ja...  16 us
    pallas_call x1, Pallas kernels, on_device(): pl.pallas_call(update_kernel, out_shape=(like((1, 1), F32), two, two, man...  1.94 us

profile of v2, /device:TPU:0, one launch (start us, length us, event | category | flops | bytes accessed | tf_op | source)
XLA Modules:
  0.0 83.2 jit_solution(4596568272510807022)
XLA Ops:
  0.6 16.0 %shard_map.346 = (bf16[4096,1024]{1,0:T(8,128)(2,1)}, bf16[32,1024]{1,0:T(8,128)(2,1)}) custom-call(s32[4]{0:T(128)} %fill.3, s32[4,1024]{1,0:T(4,128)} %ids.3, s32[4,1024]{1,0:T(4,128)} %seg.3, bf16[12568,1024]{1,0:T(8,128)(2,1)} %words.1), custom_call_target="tpu_custom_call" | custom-call | tf_op jit(solution)/shard_map/pallas_call | solution.py:241
  16.6 64.5 %shard_map.347 = (f32[32,1024]{1,0:T(8,128)}, f32[8,256]{1,0:T(8,128)}) custom-call(s32[4]{0:T(128)} %fill.3, s32[8]{0:T(128)} %task_w.1, s32[4,1024]{1,0:T(4,128)} %ids.3, s32[4,1024]{1,0:T(4,128)} %seg.3, s32[4,8]{1,0:T(4,128)} %tasks.1, s32[4,8]{1,0:T(4,128)} %labels.1, bf16[32,1024]{1,0:T(8,128)(2,1)} %get-tuple-element.28.lead_out, f32[3,1024]{1,0:T(4,128)} %gains.1, ...), custom_call_target="tpu_custom_call" | custom-call | tf_op jit(solution)/shard_map/pallas_call | solution.py:852
  81.1 1.9 %shard_map.348 = (f32[1,1]{1,0:T(1,128)}, f32[2,1024]{1,0:T(2,128)}, f32[2,1024]{1,0:T(2,128)}, f32[24,1024]{1,0:T(8,128)}, f32[2,1024]{1,0:T(2,128)}, /*index=5...) custom-call(f32[32,1024]{1,0:T(8,128)} %get-tuple-element.30.heads_s, ...), custom_call_target="tpu_custom_call" | custom-call | tf_op jit(solution)/shard_map/pallas_call | solution.py:868

commit v3 on v2

--- a/solution.py
+++ b/solution.py
@@ -403,20 +403,33 @@
     def tile_at(t):
         return pl.ds(pl.multiple_of(LANES * t, LANES), LANES)
 
-    def absorb(t, _):
-        r = mm(xl, qkv[:, pl.ds(pl.multiple_of(384 * t, LANES), 256)])
-        at = tile_at(t)
+    for t in range(PAIRS):
+        r = mm(xl, qkv[:, 384 * t : 384 * t + 256])
+        at = slice(LANES * t, LANES * (t + 1))
         q = jnp.where(low_half, r[:, :LANES], r[:, LANES:]) + (biases[0:1, at] + scale_b[0:1, at] * eq_s[:, at])
-        turned = pltpu.roll(q.astype(BF).astype(F32) * 0.125, HDIM, 1)
-        a0 = mm_t(jnp.where(low_half, 0.0, turned).astype(BF), qkv[:, tile_at(3 * t)])
-        a1 = mm_t(jnp.where(low_half, turned, 0.0).astype(BF), qkv[:, tile_at(3 * t + 2)])
-        both = pl.ds(pl.multiple_of(16 * t, 16), 16)
+        gq_s[:, at] = pltpu.roll(q.astype(BF).astype(F32) * 0.125, HDIM, 1)
+
+    def keys_at(t):
+        first = max(384 * t - LANES, 0)
+        return slice(first, min(384 * t + LANES, 3 * D))
+
+    def both_heads(t):
+        parts, none = [], jnp.zeros((L, LANES), F32)
+        if t > 0:
+            odd = jnp.where(low_half, gq_s[:, LANES * (t - 1) : LANES * t], 0.0)
+            parts.append(odd if t == PAIRS else jnp.concatenate([odd, none], 1))
+        if t < PAIRS:
+            even = jnp.where(low_half, 0.0, gq_s[:, LANES * t : LANES * (t + 1)])
+            parts.append(even if t == 0 else jnp.concatenate([none, even], 1))
+        return jnp.concatenate(parts, 0).astype(BF)
+
+    even = mm_t(both_heads(0), qkv[:, keys_at(0)])
+    for t in range(PAIRS):
+        found = mm_t(both_heads(t + 1), qkv[:, keys_at(t + 1)])
         for r_ in range(R):
             rows = slice(r_ * SEGS, (r_ + 1) * SEGS)
-            qk[r_, both, :] = jnp.concatenate([a0[rows], a1[rows]], 0).astype(BF)
-        return 0
-
-    lax.fori_loop(0, PAIRS, absorb, 0, unroll=UNROLL)
+            qk[r_, 16 * t : 16 * (t + 1), :] = jnp.concatenate([even[rows], found[:L][rows]], 0).astype(BF)
+        even = found[L:]
 
     Q = HEADS * SEGS
     qj = lax.rem(iota((Q, 1), 0), SEGS)
@@ -487,17 +500,19 @@
 
     lax.fori_loop(0, D // NT, latents, 0, unroll=D // NT)
 
+    def values_at(t):
+        return pl.ds(pl.multiple_of(LANES * (3 * t + 1), LANES), 2 * LANES)
+
     def two(t):
         return pl.ds(pl.multiple_of(2 * L * t, 2 * L), 2 * L)
 
     def values(t, _):
         at = tile_at(t)
-        v0 = mm(ub[2 * t], qkv[:, tile_at(3 * t + 1)])
-        v1 = mm(ub[2 * t + 1], qkv[:, tile_at(3 * t + 2)])
+        v = mm(ub[pl.ds(2 * t, 2)].reshape(2 * L, D), qkv[:, values_at(t)])
         pair = mm((ua[two(t), :] * scale_d[1:2, :]).astype(BF), vb[:, at])
         extra = jnp.where(low_half, pair[:L], pair[L:])
         ev[:, at] = extra
-        mixed = jnp.where(low_half, v0, v1) + scale_b[1:2, at] * extra
+        mixed = jnp.where(low_half, v[:L, :LANES], v[L:, LANES:]) + scale_b[1:2, at] * extra
         pack[:, :, at] = mixed.reshape(R, SEGS, LANES)
         return 0
 
@@ -672,9 +687,10 @@
     def back_value(t, acc):
         at = tile_at(t)
         g = g_in[:, :, at].reshape(L, LANES)
-        z0 = mm_t(jnp.where(low_half, g, 0.0).astype(BF), qkv[:, tile_at(3 * t + 1)])
-        z1 = mm_t(jnp.where(low_half, 0.0, g).astype(BF), qkv[:, tile_at(3 * t + 2)])
-        zacc[two(t), :] = jnp.concatenate([z0, z1], 0)
+        none = jnp.zeros((L, LANES), F32)
+        upper = jnp.concatenate([jnp.where(low_half, g, 0.0), none], 1)
+        lower = jnp.concatenate([none, jnp.where(low_half, 0.0, g)], 1)
+        zacc[two(t), :] = mm_t(jnp.concatenate([upper, lower], 0).astype(BF), qkv[:, values_at(t)])
         gb = g * scale_b[1:2, at]
         both = jnp.concatenate([jnp.where(low_half, gb, 0.0), jnp.where(low_half, 0.0, gb)], 0).astype(BF)
         back = mm_t(both, vb[:, at])
@@ -732,14 +748,13 @@
             c = lax.rem(z, CHUNKS)
             over("heads", d, ag.at[c], ag.at[c], ag_ss.at[d], ag_rs.at[c]).start()
 
-    def back_query(t, _):
-        at = tile_at(t)
-        k0 = mm(ub[2 * t], qkv[:, tile_at(3 * t)])
-        k1 = mm(ub[2 * t + 1], qkv[:, tile_at(3 * t + 2)])
-        gq_s[:, at] = pltpu.roll(jnp.where(low_half, k1, k0), HDIM, 1) * 0.125
-        return 0
-
-    lax.fori_loop(0, PAIRS, back_query, 0, unroll=UNROLL)
+    even = mm(ub[0], qkv[:, keys_at(0)])
+    for t in range(PAIRS):
+        heads = slice(2 * t + 1, min(2 * t + 3, HEADS))
+        found = mm(ub[heads].reshape(-1, D), qkv[:, keys_at(t + 1)])
+        both = jnp.where(low_half, found[:L, :LANES], even)
+        gq_s[:, LANES * t : LANES * (t + 1)] = pltpu.roll(both, HDIM, 1) * 0.125
+        even = found[L:, LANES:]
     g_query = gq_s[...]
     grad_b0 = jnp.sum(g_query * eq_s[...], 0, keepdims=True)
     back = mm_t((g_query * scale_b[0:1, :]).astype(BF), vb[...])

time: 83.6 us -> 81.2 us (0.971)
  Pallas kernels: 82.4 us -> 80.6 us
    pallas_call x1, Pallas kernels: 64.5 us -> 61.8 us  [on_device(): pl.pallas_call(functools.partial(step_kernel, (R, S, G, NR, V)), out_shap...]
    pallas_call x1, Pallas kernels: 16 us -> 16.9 us  [gather(): pl.pallas_call(functools.partial(gather_kernel, (R, S, V)), out_shape=(ja...]
where the time goes in v3:
time: 81.2 us; the launch traced here: 81.5 us
  Pallas kernels  80.6 us (99%)
  between operations  0.83 us (1%)
    pallas_call x1, Pallas kernels, on_device(): pl.pallas_call(functools.partial(step_kernel, (R, S, G, NR, V)), out_shap...  61.8 us
    pallas_call x1, Pallas kernels, gather(): pl.pallas_call(functools.partial(gather_kernel, (R, S, V)), out_shape=(ja...  16.9 us
    pallas_call x1, Pallas kernels, on_device(): pl.pallas_call(update_kernel, out_shape=(like((1, 1), F32), two, two, man...  1.94 us

profile of v3, /device:TPU:0, one launch (start us, length us, event | category | flops | bytes accessed | tf_op | source)
XLA Modules:
  0.0 81.5 jit_solution(9627365207653603624)
XLA Ops:
  0.6 16.9 %shard_map.346 = (bf16[4096,1024]{1,0:T(8,128)(2,1)}, bf16[32,1024]{1,0:T(8,128)(2,1)}) custom-call(s32[4]{0:T(128)} %fill.3, s32[4,1024]{1,0:T(4,128)} %ids.3, s32[4,1024]{1,0:T(4,128)} %seg.3, bf16[12568,1024]{1,0:T(8,128)(2,1)} %words.1), custom_call_target="tpu_custom_call" | custom-call | tf_op jit(solution)/shard_map/pallas_call | solution.py:241
  17.6 61.8 %shard_map.347 = (f32[32,1024]{1,0:T(8,128)}, f32[8,256]{1,0:T(8,128)}) custom-call(s32[4]{0:T(128)} %fill.3, s32[8]{0:T(128)} %task_w.1, s32[4,1024]{1,0:T(4,128)} %ids.3, s32[4,1024]{1,0:T(4,128)} %seg.3, s32[4,8]{1,0:T(4,128)} %tasks.1, s32[4,8]{1,0:T(4,128)} %labels.1, bf16[32,1024]{1,0:T(8,128)(2,1)} %get-tuple-element.28.lead_out, f32[3,1024]{1,0:T(4,128)} %gains.1, ...), custom_call_target="tpu_custom_call" | custom-call | tf_op jit(solution)/shard_map/pallas_call | solution.py:867
  79.4 1.9 %shard_map.348 = (f32[1,1]{1,0:T(1,128)}, f32[2,1024]{1,0:T(2,128)}, f32[2,1024]{1,0:T(2,128)}, f32[24,1024]{1,0:T(8,128)}, f32[2,1024]{1,0:T(2,128)}, /*index=5...) custom-call(f32[32,1024]{1,0:T(8,128)} %get-tuple-element.30.heads_s, ...), custom_call_target="tpu_custom_call" | custom-call | tf_op jit(solution)/shard_map/pallas_call | solution.py:883

commit v4 on v3

--- a/solution.py
+++ b/solution.py
@@ -677,12 +677,18 @@
 
     holder = None if G == CHUNKS else z < CHUNKS
     take_in(0, lse_out, lse_in)
+    scale = [jnp.exp(st[r] - lse_in[r]) for r in range(R)]
+    factor = jnp.concatenate([jnp.where(lane < HEADS, s, 0.0) for s in scale], 0)
+    ev[...] = ev[...] * expand(factor)
+    for r in range(R):
+        f = to_col(factor[r * SEGS : (r + 1) * SEGS])
+        for c in range(0, Q, PART):
+            rows = slice(c, c + PART)
+            expo[r][rows, :] = expo[r][rows, :] * f[rows]
     take_in(1, gpk, gpk_in)
     for r in range(R):
         g_in[r] = widen(gpk_in[r])
 
-    scale = [jnp.exp(st[r] - lse_in[r]) for r in range(R)]
-    factor = jnp.concatenate([jnp.where(lane < HEADS, s, 0.0) for s in scale], 0)
 
     def back_value(t, acc):
         at = tile_at(t)
@@ -701,7 +707,7 @@
         return acc
 
     grad_d1 = lax.fori_loop(0, PAIRS, back_value, jnp.zeros((1, D), F32), unroll=UNROLL)
-    grad_b1 = jnp.sum(g_in[...].reshape(L, D) * ev[...] * expand(factor), 0, keepdims=True)
+    grad_b1 = jnp.sum(g_in[...].reshape(L, D) * ev[...], 0, keepdims=True)
     extra = TASKS * CLASSES + 1
     hs[extra : extra + 2, :] = jnp.concatenate([grad_d1, grad_b1], 0)
     spread(chunk_of, lambda d: h_in.at[d], h_ss, lambda d: h_rs.at[d], small, lambda c: c.start())
@@ -728,11 +734,10 @@
         gdot[r % 2][...] = mm_t(zq[r], rows_of(r))
 
     def bend(r):
-        f = to_col(jnp.where(lane < HEADS, jnp.exp(st[r] - lse_in[r]), 0.0))
         delta = to_col(dlt_in[r])
         for c in range(0, Q, PART):
             rows = slice(c, c + PART)
-            ds = (expo[r][rows, :] * f[rows]) * (gdot[r % 2][rows, :] - delta[rows])
+            ds = expo[r][rows, :] * (gdot[r % 2][rows, :] - delta[rows])
             low[r][rows, :] = ds.astype(BF)
 
     take_in(2, dlt_out, dlt_in)

time: 81.2 us -> 81.5 us (level)
    pallas_call x1, Pallas kernels: 16.9 us -> 15.4 us  [gather(): pl.pallas_call(functools.partial(gather_kernel, (R, S, V)), out_shape=(ja...]
    pallas_call x1, Pallas kernels: 61.8 us -> 63.2 us  [on_device(): pl.pallas_call(functools.partial(step_kernel, (R, S, G, NR, V)), out_shap...]
where the time goes in v4:
time: 81.5 us; the launch traced here: 81.3 us
  Pallas kernels  80.5 us (99%)
  between operations  0.83 us (1%)
    pallas_call x1, Pallas kernels, on_device(): pl.pallas_call(functools.partial(step_kernel, (R, S, G, NR, V)), out_shap...  63.2 us
    pallas_call x1, Pallas kernels, gather(): pl.pallas_call(functools.partial(gather_kernel, (R, S, V)), out_shape=(ja...  15.4 us
    pallas_call x1, Pallas kernels, on_device(): pl.pallas_call(update_kernel, out_shape=(like((1, 1), F32), two, two, man...  1.94 us

profile of v4, /device:TPU:0, one launch (start us, length us, event | category | flops | bytes accessed | tf_op | source)
XLA Modules:
  0.0 81.3 jit_solution(17911175997657346617)
XLA Ops:
  0.6 15.4 %shard_map.346 = (bf16[4096,1024]{1,0:T(8,128)(2,1)}, bf16[32,1024]{1,0:T(8,128)(2,1)}) custom-call(s32[4]{0:T(128)} %fill.3, s32[4,1024]{1,0:T(4,128)} %ids.3, s32[4,1024]{1,0:T(4,128)} %seg.3, bf16[12568,1024]{1,0:T(8,128)(2,1)} %words.1), custom_call_target="tpu_custom_call" | custom-call | tf_op jit(solution)/shard_map/pallas_call | solution.py:241
  16.0 63.2 %shard_map.347 = (f32[32,1024]{1,0:T(8,128)}, f32[8,256]{1,0:T(8,128)}) custom-call(s32[4]{0:T(128)} %fill.3, s32[8]{0:T(128)} %task_w.1, s32[4,1024]{1,0:T(4,128)} %ids.3, s32[4,1024]{1,0:T(4,128)} %seg.3, s32[4,8]{1,0:T(4,128)} %tasks.1, s32[4,8]{1,0:T(4,128)} %labels.1, bf16[32,1024]{1,0:T(8,128)(2,1)} %get-tuple-element.28.lead_out, f32[3,1024]{1,0:T(4,128)} %gains.1, ...), custom_call_target="tpu_custom_call" | custom-call | tf_op jit(solution)/shard_map/pallas_call | solution.py:872
  79.2 1.9 %shard_map.348 = (f32[1,1]{1,0:T(1,128)}, f32[2,1024]{1,0:T(2,128)}, f32[2,1024]{1,0:T(2,128)}, f32[24,1024]{1,0:T(8,128)}, f32[2,1024]{1,0:T(2,128)}, /*index=5...) custom-call(f32[32,1024]{1,0:T(8,128)} %get-tuple-element.30.heads_s, ...), custom_call_target="tpu_custom_call" | custom-call | tf_op jit(solution)/shard_map/pallas_call | solution.py:888
